TPU v7x, 512 devices: a whole 4x4x16 slice. The times are simulated.
512 devices in a mesh: row: 16 (over z_lo, y), col: 32 (over x, z_hi, core).
Axes of the slice: x: 4, y: 4, z: 16 (z_hi: 4, z_lo: 4; z = z_hi * 4 + z_lo), core: 2. Of those that a mesh axis runs over, the one named last changes fastest.
Arguments:
- hidden: bfloat16 [1024, 24576], P('col', 'row'), may hold values from -0.75 to 0.75
- weight: bfloat16 [24576, 12288], P('row', 'col'), may hold values from -0.0390625 to 0.0390625
- out_grad: bfloat16 [1024, 12288], P('row', 'col'), may hold values from -1.5 to 1.5
Outputs:
- input_grad: bfloat16 [1024, 24576], P('col', 'row')
- weight_grad: bfloat16 [24576, 12288], P('row', 'col')
All inputs are finite; a program needn't handle non-finite values.
Results may differ from a plain program's by a relative error of at most 0.019.
Values may be sent and summed in bfloat16 or wider, within the bound.
A program may use at most 64 MiB of HBM per device.

v0:
```python
import jax
import jax.numpy as jnp
from jax import lax
from jax.sharding import PartitionSpec as P


def shards(hidden, weight, out_grad):
    grads_all = lax.all_gather(out_grad, "row", axis=0, tiled=True)
    grad_rows = grads_all
    weight_grad = lax.dot_general(
        lax.all_gather(hidden, "col", axis=0, tiled=True),
        grad_rows,
        (((0,), (0,)), ((), ())),
        preferred_element_type=jnp.float32,
    ).astype(jnp.bfloat16)
    grad_rows = grads_all
    input_grad = lax.psum_scatter(
        lax.dot_general(
            grad_rows, weight, (((1,), (1,)), ((), ())), preferred_element_type=jnp.float32
        ).astype(jnp.bfloat16),
        "col",
        scatter_dimension=0,
        tiled=True,
    )
    return (input_grad, weight_grad)


def solution(mesh):
    in_specs = (P("col", "row"), P("row", "col"), P("row", "col"))
    out_specs = (P("col", "row"), P("row", "col"))
    return jax.shard_map(shards, mesh=mesh, in_specs=in_specs, out_specs=out_specs, check_vma=False)
```

profile of v0, /device:TPU:1, one launch (start us, length us, event | category | flops | bytes accessed | tf_op | source)
XLA Modules:
  0.0 241.0 jit_solution(17998017359407155877)
XLA Ops:
  7.2 0.0 copy-start
  7.2 0.0 all-gather.2.cloned.1.call-start
  7.2 0.7 all-gather.2.cloned.1.call-update
  7.9 0.0 reduce-scatter.2.cloned.1.call-start
  8.0 44.7 %all_gather.6 = bf16[1024,384]{1,0:T(8,128)(2,1)S(1)} all-gather(bf16[64,384]{1,0:T(8,128)(2,1)} %param.5), channel_id=1, replica_groups=mesh['row'=16,'col'=32] {'row'}, dimensions={0}, use_global_device_ids=true | all-gather | bytes 835584 | tf_op jit(solution)/shard_map/all_gather | solution.py:8
  52.7 0.0 copy-done
  52.7 3.5 %convolution_convert_fusion = bf16[1024,1536]{1,0:T(8,128)(2,1)} fusion(bf16[1024,384]{1,0:T(8,128)(2,1)S(1)} %all_gather.6, bf16[1536,384]{1,0:T(8,128)(2,1)S(1)} %copy-done), kind=kOutput, calls=%fused_computation | convolution fusion | flops 1209532416 | bytes 5111808 | tf_op jit(solution)/shard_map/dot_general | solution.py:18
  56.2 0.0 reduce-scatter.2.cloned.1.call-update
  56.2 48.9 %all-gather.2.cloned.1.call-done = bf16[1024,1536]{1,0:T(8,128)(2,1)} async-done(((bf16[32,1536]{1,0:T(8,128)(2,1)}), bf16[1024,1536]{1,0:T(8,128)(2,1)}) %all-gather.2.cloned.1.call-update) | async-done | bytes 3145744 | tf_op jit(solution)/shard_map/all_gather | solution.py:11
  105.1 4.7 %convolution_convert_fusion.1 = bf16[1536,384]{1,0:T(8,128)(2,1)} fusion(bf16[1024,1536]{1,0:T(8,128)(2,1)} %all-gather.2.cloned.1.call-done, bf16[1024,384]{1,0:T(8,128)(2,1)S(1)} %all_gather.6), kind=kOutput, calls=%fused_computation.1 | convolution fusion | flops 1208549376 | bytes 5111808 | tf_op jit(solution)/shard_map/dot_general | solution.py:10
  109.8 124.4 %reduce-scatter.2.cloned.1.call-done = bf16[32,1536]{1,0:T(8,128)(2,1)} async-done(((bf16[1024,1536]{1,0:T(8,128)(2,1)}), bf16[32,1536]{1,0:T(8,128)(2,1)}) %reduce-scatter.2.cloned.1.call-update) | async-done | bytes 98320 | tf_op jit(solution)/shard_map/reduce_scatter | solution.py:17
Async XLA Ops:
  7.2 45.5 %copy-start = (bf16[1536,384]{1,0:T(8,128)(2,1)S(1)}, bf16[1536,384]{1,0:T(8,128)(2,1)}, u32[]{:S(2)}) copy-start(bf16[1536,384]{1,0:T(8,128)(2,1)} %param.4) | copy-start | bytes 3538948
  7.2 97.9 %all-gather.2.cloned.1.call-start = ((), (), s32[]{:S(2)}) async-start(), calls=%async_computation.2 | async-start | bytes 3244032 | tf_op jit(solution)/shard_map/all_gather | solution.py:11
  7.9 226.3 %reduce-scatter.2.cloned.1.call-start = ((), (), s32[]{:S(2)}) async-start(), calls=%async_computation.1 | async-start | bytes 3244032 | tf_op jit(solution)/shard_map/reduce_scatter | solution.py:17
Sparse Core Ops, SparseCore 0:
  11.1 93.8 all-gather.1
  110.2 123.9 reduce-scatter.1
where the time goes:
time: 241 us
  waiting for transfers between devices  174 us (72%)
  blocking collectives  44.7 us (19%)
  between operations  14 us (6%)
  matrix products  8.23 us (3%)
    reduce_scatter x1, waiting for transfers between devices, shards(): lax.psum_scatter(lax.dot_general(grad_rows, weight, (((1,), (1,)), ((), (...  124 us
    all_gather x1, waiting for transfers between devices, shards(): lax.all_gather(hidden, 'col', axis=0, tiled=True)  48.9 us
    all_gather x1, blocking collectives, shards(): grads_all = lax.all_gather(out_grad, 'row', axis=0, tiled=True)  44.7 us
  transfers between devices with their start and end apart: 2, of which 2 were waited for; matrix products, arithmetic and copies ran while one was open for 3% of the time, Pallas kernels for 0%

commit v1 on v0

v1 whole, which is shorter than its diff:
```python
import jax
import jax.numpy as jnp
from jax import lax
from jax.experimental import pallas as pl
from jax.experimental.pallas import tpu as pltpu
from jax.sharding import PartitionSpec as P

BF16, F32 = jnp.bfloat16, jnp.float32
FF, D, T = 1536, 384, 32
A, B = pl.ds(0, T // 2), pl.ds(T // 2, T // 2)
SENDS = 96


def kernel(
    h_ref, w_ref, g_ref, ig_ref, wg_ref,
    hall, gall, gsib, wall, part, ra, rb, r2p, r2m, summed, za, zb, z2p, z2m, acc,
    send_sem, recv_sem, local_sem,
):
    r, c = lax.axis_index("row"), lax.axis_index("col")
    zl, y = r // 4, r % 4
    x, zh, k = c // 8, (c // 2) % 4, c % 2

    def at(dzl=0, dy=0, dx=0, dzh=0, dk=0):
        row = ((zl + dzl) % 4) * 4 + (y + dy) % 4
        col = (((x + dx) % 4) * 4 + (zh + dzh) % 4) * 2 + (k + dk) % 2
        return (row, col)

    started = []

    def send(src, dst, to):
        i = len(started)
        copy = pltpu.make_async_remote_copy(
            src_ref=src, dst_ref=dst, send_sem=send_sem.at[i], recv_sem=recv_sem.at[i],
            device_id=to, device_id_type=pl.DeviceIdType.MESH,
        )
        copy.start()
        started.append(copy)
        return copy

    load_w = pltpu.make_async_copy(w_ref, wall.at[:, pl.ds(0, D)], local_sem.at[0])
    load_g = pltpu.make_async_copy(g_ref, gall.at[y, zl], local_sem.at[1])
    load_h = pltpu.make_async_copy(h_ref, hall.at[zh, x, k], local_sem.at[2])
    for load in (load_g, load_h, load_w):
        load.start()

    partners = [at(dzl=1), at(dzl=2), at(dzl=3), at(dy=1), at(dy=2), at(dy=3)]
    partners += [at(dx=1), at(dx=3), at(dzh=1), at(dzh=3), at(dk=1)]
    barrier = pltpu.get_barrier_semaphore()
    for partner in partners:
        pl.semaphore_signal(barrier, inc=1, device_id=partner, device_id_type=pl.DeviceIdType.MESH)
    pl.semaphore_wait(barrier, len(partners))

    right, left, up, down, sib = at(dx=1), at(dx=3), at(dzh=1), at(dzh=3), at(dk=1)
    xr, xl, x2 = (x + 1) % 4, (x + 3) % 4, (x + 2) % 4
    zu, zd, z2 = (zh + 1) % 4, (zh + 3) % 4, (zh + 2) % 4

    g_zl = {d: send(g_ref, gall.at[y, zl], at(dzl=d)) for d in (1, 3, 2)}
    g_y = {(0, d): send(g_ref, gall.at[y, zl], at(dy=d)) for d in (1, 3, 2)}
    w_sib = send(w_ref, wall.at[:, pl.ds(D, D)], sib)
    hz_a = send(h_ref.at[A], hall.at[zh, x, k, A], up)
    hz_b = send(h_ref.at[B], hall.at[zh, x, k, B], down)
    hx = {}
    load_h.wait()

    def h_x_half(q, zq, half):
        block = hall.at[zq, x, k, half]
        hx[q, "a" if half is A else "b", "r"] = send(block, block, right)
        hx[q, "a" if half is A else "b", "l"] = send(block, block, left)

    def h_x_forward(q, zq):
        hx[q, "a", "r"].wait_recv()
        block = hall.at[zq, xl, k, A]
        hx[q, "fa"] = send(block, block, right)
        hx[q, "b", "l"].wait_recv()
        block = hall.at[zq, xr, k, B]
        hx[q, "fb"] = send(block, block, left)

    def h_x_end(q, zq):
        for name in ((q, "b", "r"), (q, "a", "l"), (q, "fa"), (q, "fb")):
            hx[name].wait_recv()
        block = hall.at[zq, :, k]
        hx[q, "sib"] = send(block, block, sib)

    h_x_half(0, zh, A)
    h_x_half(0, zh, B)
    hz_a2 = send(h_ref.at[B], hall.at[zh, x, k, B], up)
    hz_b2 = send(h_ref.at[A], hall.at[zh, x, k, A], down)

    for d in (1, 3, 2):
        g_zl[d].wait_recv()
        block = gall.at[y, (zl - d + 4) % 4]
        for dy in (1, 3, 2):
            g_y[d, dy] = send(block, block, at(dy=dy))
    load_g.wait()

    def g_to_sib(b):
        return send(gall.at[b, :, 1 - k], gsib.at[b], sib)

    g_sib = [g_to_sib(y)]
    h_x_forward(0, zh)
    load_w.wait()
    w_sib.wait_recv()

    bs = [y, (y + 3) % 4, (y + 1) % 4, (y + 2) % 4]
    rs = {}

    def reduce_x_start(j):
        b = bs[j]
        g_sib[j].wait_recv()
        grads = jnp.concatenate([gall[b, :, k].reshape(4 * T, D), gsib[b].reshape(4 * T, D)], axis=1)
        for n in range(0, FF, 512):
            cols = pl.ds(n, 512)
            block = lax.dot_general(grads, wall[cols], (((1,), (1,)), ((), ())), preferred_element_type=F32)
            part[j, :, :, cols] = block.astype(BF16).reshape(4, T, 512)
        rs[j, "1a"] = send(part.at[j, x2, A], ra.at[j], right)
        rs[j, "1b"] = send(part.at[j, x2, B], rb.at[j], left)
        rs[j, "2a"] = send(part.at[j, xr, B], r2p.at[j, B], right)
        rs[j, "2b"] = send(part.at[j, xl, A], r2m.at[j, A], left)

    def reduce_x_forward(j):
        rs[j, "1a"].wait_recv()
        part[j, xr, A] = (part[j, xr, A].astype(F32) + ra[j].astype(F32)).astype(BF16)
        rs[j, "2c"] = send(part.at[j, xr, A], r2p.at[j, A], right)
        rs[j, "1b"].wait_recv()
        part[j, xl, B] = (part[j, xl, B].astype(F32) + rb[j].astype(F32)).astype(BF16)
        rs[j, "2d"] = send(part.at[j, xl, B], r2m.at[j, B], left)

    def reduce_x_end(j):
        for name in ("2a", "2b", "2c", "2d"):
            rs[j, name].wait_recv()
        summed[bs[j]] = (part[j, x].astype(F32) + r2p[j].astype(F32) + r2m[j].astype(F32)).astype(BF16)

    reduce_x_start(0)
    hz_a.wait_recv()
    hz_fa = send(hall.at[zd, x, k, A], hall.at[zd, x, k, A], up)
    hz_b.wait_recv()
    hz_fb = send(hall.at[zu, x, k, B], hall.at[zu, x, k, B], down)
    for j, d in ((1, 1), (2, 3), (3, 2)):
        for e in (0, 1, 3, 2):
            g_y[e, d].wait_recv()
        g_sib.append(g_to_sib(bs[j]))
        reduce_x_forward(j - 1)
        reduce_x_start(j)
    h_x_end(0, zh)
    reduce_x_forward(3)

    def weight_grad(q, zq):
        hx[q, "sib"].wait_recv()
        grads = gall[zq].reshape(8 * T, D)
        for m in range(0, FF, 512):
            rows = pl.ds(m, 512)
            block = lax.dot_general(
                hall[zq, :, :, :, rows].reshape(8 * T, 512), grads, (((0,), (0,)), ((), ())), preferred_element_type=F32
            )
            if q == 0:
                acc[rows] = block
            elif q < 3:
                acc[rows] += block
            else:
                wg_ref[rows] = (acc[rows] + block).astype(BF16)

    hz_b2.wait_recv()
    hz_a2.wait_recv()
    h_x_half(1, zd, A)
    h_x_half(1, zd, B)
    h_x_half(2, zu, A)
    h_x_half(2, zu, B)

    for j in range(4):
        reduce_x_end(j)
    z1a = send(summed.at[z2, A], za, up)
    z1b = send(summed.at[z2, B], zb, down)
    z2a = send(summed.at[zu, B], z2p.at[B], up)
    z2b = send(summed.at[zd, A], z2m.at[A], down)
    weight_grad(0, zh)
    hz_fa.wait_recv()
    h_x_half(3, z2, A)
    hz_fb.wait_recv()
    h_x_half(3, z2, B)
    h_x_forward(1, zd)
    h_x_forward(2, zu)

    z1a.wait_recv()
    summed[zu, A] = (summed[zu, A].astype(F32) + za[...].astype(F32)).astype(BF16)
    z2c = send(summed.at[zu, A], z2p.at[A], up)
    z1b.wait_recv()
    summed[zd, B] = (summed[zd, B].astype(F32) + zb[...].astype(F32)).astype(BF16)
    z2d = send(summed.at[zd, B], z2m.at[B], down)

    h_x_forward(3, z2)
    h_x_end(1, zd)
    h_x_end(2, zu)
    weight_grad(1, zd)
    weight_grad(2, zu)
    h_x_end(3, z2)
    weight_grad(3, z2)

    for copy in (z2a, z2b, z2c, z2d):
        copy.wait_recv()
    ig_ref[...] = (summed[zh].astype(F32) + z2p[...].astype(F32) + z2m[...].astype(F32)).astype(BF16)
    for copy in started:
        copy.wait_send()


def shards(hidden, weight, out_grad):
    vmem = lambda *shape, dtype=BF16: pltpu.VMEM(shape, dtype)
    return pl.pallas_call(
        kernel,
        name="mlp_backward",
        out_shape=(jax.ShapeDtypeStruct((T, FF), BF16), jax.ShapeDtypeStruct((FF, D), BF16)),
        in_specs=[pl.BlockSpec(memory_space=pl.ANY)] * 3,
        out_specs=[pl.BlockSpec(memory_space=pltpu.VMEM)] * 2,
        scratch_shapes=[
            vmem(4, 4, 2, T, FF),
            vmem(4, 4, 2, T, D),
            vmem(4, 4, T, D),
            vmem(FF, 2 * D),
            vmem(4, 4, T, FF),
            vmem(4, T // 2, FF), vmem(4, T // 2, FF),
            vmem(4, T, FF), vmem(4, T, FF),
            vmem(4, T, FF),
            vmem(T // 2, FF), vmem(T // 2, FF),
            vmem(T, FF), vmem(T, FF),
            vmem(FF, D, dtype=F32),
            pltpu.SemaphoreType.DMA((SENDS,)),
            pltpu.SemaphoreType.DMA((SENDS,)),
            pltpu.SemaphoreType.DMA((3,)),
        ],
        compiler_params=pltpu.CompilerParams(
            collective_id=0, has_side_effects=True, vmem_limit_bytes=48 << 20
        ),
        cost_estimate=pl.CostEstimate(flops=2416 << 20, bytes_accessed=4 << 20, transcendentals=0),
    )(hidden, weight, out_grad.reshape(2, T, D))


def solution(mesh):
    in_specs = (P("col", "row"), P("row", "col"), P("row", "col"))
    out_specs = (P("col", "row"), P("row", "col"))
    return jax.shard_map(shards, mesh=mesh, in_specs=in_specs, out_specs=out_specs, check_vma=False)
```

time: 241 us -> 75.3 us (0.31)
  the two profiles are of different devices: /device:TPU:1 before, /device:TPU:65 now
where the time goes in v1:
time: 75.3 us; the launch traced here: 75.1 us
  Pallas kernels  69.9 us (93%)
  local copies, waits for them, and re-layouts  4.61 us (6%)
    pallas_call x1, Pallas kernels, shards(): pl.pallas_call(kernel, name='mlp_backward', out_shape=(jax.ShapeDtypeStru...  69.9 us
    unnamed x8, local copies, waits for them, and re-layouts  4.61 us

profile of v1, /device:TPU:65, one launch (start us, length us, event | category | flops | bytes accessed | tf_op | source)
XLA Modules:
  0.0 75.1 jit_solution(16002747982434234439)
XLA Ops:
  0.6 0.0 copy-start
  0.6 1.3 %copy-done = bf16[1536,384]{1,0:T(8,128)(2,1)S(1)} copy-done((bf16[1536,384]{1,0:T(8,128)(2,1)S(1)}, bf16[1536,384]{1,0:T(8,128)(2,1)}, u32[]{:S(2)}) %copy-start) | copy-done | bytes 1179672
  1.9 0.0 copy-start.1
  1.9 0.9 %copy-done.1 = bf16[32,1536]{1,0:T(8,128)(2,1)S(1)} copy-done((bf16[32,1536]{1,0:T(8,128)(2,1)S(1)}, bf16[32,1536]{1,0:T(8,128)(2,1)}, u32[]{:S(2)}) %copy-start.1) | copy-done | bytes 98328
  2.8 0.0 copy-start.2
  2.8 0.8 %copy-done.2 = bf16[64,384]{1,0:T(8,128)(2,1)S(1)} copy-done((bf16[64,384]{1,0:T(8,128)(2,1)S(1)}, bf16[64,384]{1,0:T(8,128)(2,1)}, u32[]{:S(2)}) %copy-start.2) | copy-done | bytes 49176
  3.6 69.9 %mlp_backward.1 = (bf16[32,1536]{1,0:T(8,128)(2,1)S(1)}, bf16[1536,384]{1,0:T(8,128)(2,1)S(1)}) custom-call(bf16[32,1536]{1,0:T(8,128)(2,1)S(1)} %copy-done.1, bf16[1536,384]{1,0:T(8,128)(2,1)S(1)} %copy-done, bf16[2,32,384]{2,1,0:T(8,128)(2,1)S(1)} %bitcast.1), custom_call_target="tpu_custom_call" | custom-call | flops 2533359616 | bytes 4194304 | tf_op jit(solution)/shard_map/mlp_backward/pallas_call | solution.py:207
  73.5 0.6 copy.7
  74.1 1.0 %copy.8 = bf16[1536,384]{1,0:T(8,128)(2,1)} copy(bf16[1536,384]{1,0:T(8,128)(2,1)S(1)} %get-tuple-element.5) | data formatting | bytes 2359296
Async XLA Ops:
  0.6 1.3 %copy-start = (bf16[1536,384]{1,0:T(8,128)(2,1)S(1)}, bf16[1536,384]{1,0:T(8,128)(2,1)}, u32[]{:S(2)}) copy-start(bf16[1536,384]{1,0:T(8,128)(2,1)} %w_ref.1) | copy-start | bytes 3538948
  1.9 0.9 %copy-start.1 = (bf16[32,1536]{1,0:T(8,128)(2,1)S(1)}, bf16[32,1536]{1,0:T(8,128)(2,1)}, u32[]{:S(2)}) copy-start(bf16[32,1536]{1,0:T(8,128)(2,1)} %h_ref.1) | copy-start | bytes 294916
  2.8 0.8 %copy-start.2 = (bf16[64,384]{1,0:T(8,128)(2,1)S(1)}, bf16[64,384]{1,0:T(8,128)(2,1)}, u32[]{:S(2)}) copy-start(bf16[64,384]{1,0:T(8,128)(2,1)} %param.5) | copy-start | bytes 147460

commit v2 on v1

v2 whole, which is shorter than its diff:
```python
import jax
import jax.numpy as jnp
from jax import lax
from jax.experimental import pallas as pl
from jax.experimental.pallas import tpu as pltpu
from jax.sharding import PartitionSpec as P

BF16, F32 = jnp.bfloat16, jnp.float32
FF, D, T = 1536, 384, 32
A, B = pl.ds(0, T // 2), pl.ds(T // 2, T // 2)
SENDS = 84
ORDER = [('hx', 0, 'a'), ('hx', 0, 'b'), ('gy', 1), ('gy', 3), ('gy', 2), ('gs', 0), ('hxf', 0, 'a'), ('hxf', 0, 'b'), ('p', 0), ('rx', 0), ('hz1',), ('gs', 1), ('gs', 3), ('gs', 2), ('rf', 0), ('p', 1), ('rx', 1), ('hzf',), ('hz2',), ('hx', 1, 'a'), ('hx', 2, 'b'), ('p', 2), ('rx', 2), ('re', 0), ('rf', 1), ('hxf', 1, 'a'), ('hxf', 2, 'b'), ('p', 3), ('rx', 3), ('re', 1), ('rz', '1'), ('rf', 2), ('hs', 0), ('hx', 1, 'b'), ('hx', 2, 'a'), ('re', 2), ('rz', '2b'), ('rf', 3), ('hx', 3, 'a'), ('hx', 3, 'b'), ('hxf', 1, 'b'), ('hxf', 2, 'a'), ('re', 3), ('rz', '2a'), ('hs', 1), ('hs', 2), ('wg', 0), ('rz', '2c'), ('rz', '2d'), ('hxf', 3, 'a'), ('hxf', 3, 'b'), ('wg', 1), ('wg', 2), ('hs', 3), ('wg', 3)]


def kernel(
    h_ref, w_ref, g_ref, ig_ref, wg_ref,
    hall, gall, gsib, wall, part, ra, rb, r2p, r2m, summed, za, zb, z2p, z2m, acc,
    send_sem, recv_sem, local_sem, near_sem, far_sem,
):
    r, c = lax.axis_index("row"), lax.axis_index("col")
    zl, y = r // 4, r % 4
    x, zh, k = c // 8, (c // 2) % 4, c % 2

    def at(dzl=0, dy=0, dx=0, dzh=0, dk=0):
        row = ((zl + dzl) % 4) * 4 + (y + dy) % 4
        col = (((x + dx) % 4) * 4 + (zh + dzh) % 4) * 2 + (k + dk) % 2
        return (row, col)

    started = []

    def send(src, dst, to):
        i = len(started)
        copy = pltpu.make_async_remote_copy(
            src_ref=src, dst_ref=dst, send_sem=send_sem.at[i], recv_sem=recv_sem.at[i],
            device_id=to, device_id_type=pl.DeviceIdType.MESH,
        )
        copy.start()
        started.append(copy)
        return copy

    load_w = pltpu.make_async_copy(w_ref, wall.at[:, pl.ds(0, D)], local_sem.at[0])
    load_g = pltpu.make_async_copy(g_ref, gall.at[y, zl], local_sem.at[1])
    load_h = pltpu.make_async_copy(h_ref, hall.at[zh, x, k], local_sem.at[2])
    for load in (load_g, load_h, load_w):
        load.start()

    barrier = pltpu.get_barrier_semaphore()

    def signal(semaphore, to):
        pl.semaphore_signal(semaphore, inc=1, device_id=to, device_id_type=pl.DeviceIdType.MESH)

    near = [dict(dzl=1), dict(dzl=2), dict(dzl=3), dict(dy=1), dict(dy=2), dict(dy=3), dict(dx=1), dict(dx=3)]
    for chip in near:
        signal(barrier, at(dk=1 - k, **chip))
    for chip in (dict(dzh=1), dict(dzh=3)):
        signal(barrier, at(dk=k, **chip))

    @pl.when(k == 0)
    def _():
        signal(barrier, at(dk=1))

    @pl.when(k == 1)
    def _():
        pl.semaphore_wait(barrier, 2 * len(near) + 1)
        signal(near_sem, at(dk=1))

    @pl.when(k == 0)
    def _():
        pl.semaphore_wait(near_sem, 1)

    right, left, up, down, sib = at(dx=1), at(dx=3), at(dzh=1), at(dzh=3), at(dk=1)
    xr, xl, x2 = (x + 1) % 4, (x + 3) % 4, (x + 2) % 4
    zu, zd, z2 = (zh + 1) % 4, (zh + 3) % 4, (zh + 2) % 4

    g_zl = {d: send(g_ref, gall.at[y, zl], at(dzl=d)) for d in (1, 3, 2)}
    g_y = {(0, d): send(g_ref, gall.at[y, zl], at(dy=d)) for d in (1, 3, 2)}
    w_sib = send(w_ref, wall.at[:, pl.ds(D, D)], sib)
    hx, rs, g_sib, hz, rz = {}, {}, {}, {}, {}
    load_h.wait()

    far = [z2, zd, zu, zh]
    at_y = jnp.where(y == z2, 0, jnp.where(y == zd, 1, jnp.where(y == zu, 2, 3)))
    bs = [y] + [jnp.where(i < at_y, far[i], far[i + 1]) for i in range(3)]
    zq = [zh, zd, zu, z2]

    def g_along_y(d):
        g_zl[d].wait_recv()
        block = gall.at[y, (zl - d + 4) % 4]
        for dy in (1, 3, 2):
            g_y[d, dy] = send(block, block, at(dy=dy))

    def g_to_sib(d):
        if d == 0:
            load_g.wait()
        else:
            for e in (0, 1, 3, 2):
                g_y[e, d].wait_recv()
        b = (y - d + 4) % 4
        g_sib[d] = send(gall.at[b, :, 1 - k], gsib.at[b], sib)

    def h_z_first():
        @pl.when(k == 0)
        def _():
            pl.semaphore_wait(barrier, 4)
            signal(far_sem, at(dk=1))

        @pl.when(k == 1)
        def _():
            pl.semaphore_wait(far_sem, 1)

        hz["1u"] = send(h_ref.at[A], hall.at[zh, x, k, A], up)
        hz["1d"] = send(h_ref.at[B], hall.at[zh, x, k, B], down)

    def h_z_second():
        hz["2u"] = send(h_ref.at[B], hall.at[zh, x, k, B], up)
        hz["2d"] = send(h_ref.at[A], hall.at[zh, x, k, A], down)

    def h_z_forward():
        hz["1u"].wait_recv()
        hz["fa"] = send(hall.at[zd, x, k, A], hall.at[zd, x, k, A], up)
        hz["1d"].wait_recv()
        hz["fb"] = send(hall.at[zu, x, k, B], hall.at[zu, x, k, B], down)

    def h_x(q, name):
        after = {(1, "b"): "2u", (2, "a"): "2d", (3, "a"): "fa", (3, "b"): "fb"}.get((q, name))
        if after:
            hz[after].wait_recv()
        block = hall.at[zq[q], x, k, A if name == "a" else B]
        hx[q, name, "r"] = send(block, block, right)
        hx[q, name, "l"] = send(block, block, left)

    def h_x_forward(q, name):
        hx[q, name, "r" if name == "a" else "l"].wait_recv()
        block = hall.at[zq[q], xl, k, A] if name == "a" else hall.at[zq[q], xr, k, B]
        hx[q, "f" + name] = send(block, block, right if name == "a" else left)

    def h_to_sib(q):
        for name in ((q, "b", "r"), (q, "a", "l"), (q, "fa"), (q, "fb")):
            hx[name].wait_recv()
        block = hall.at[zq[q], :, k]
        hx[q, "sib"] = send(block, block, sib)

    def product(j):
        if j == 0:
            load_w.wait()
            w_sib.wait_recv()
            g_sib[0].wait_recv()
        if j == 1:
            for d in (1, 3, 2):
                g_sib[d].wait_recv()
        b = bs[j]
        grads = jnp.concatenate([gall[b, :, k].reshape(4 * T, D), gsib[b].reshape(4 * T, D)], axis=1)
        for n in range(0, FF, 512):
            cols = pl.ds(n, 512)
            block = lax.dot_general(grads, wall[cols], (((1,), (1,)), ((), ())), preferred_element_type=F32)
            part[j, :, :, cols] = block.astype(BF16).reshape(4, T, 512)

    def reduce_x(j):
        rs[j, "1a"] = send(part.at[j, x2, A], ra.at[j], right)
        rs[j, "1b"] = send(part.at[j, x2, B], rb.at[j], left)
        rs[j, "2a"] = send(part.at[j, xr, B], r2p.at[j, B], right)
        rs[j, "2b"] = send(part.at[j, xl, A], r2m.at[j, A], left)

    def reduce_x_forward(j):
        rs[j, "1a"].wait_recv()
        part[j, xr, A] = (part[j, xr, A].astype(F32) + ra[j].astype(F32)).astype(BF16)
        rs[j, "2c"] = send(part.at[j, xr, A], r2p.at[j, A], right)
        rs[j, "1b"].wait_recv()
        part[j, xl, B] = (part[j, xl, B].astype(F32) + rb[j].astype(F32)).astype(BF16)
        rs[j, "2d"] = send(part.at[j, xl, B], r2m.at[j, B], left)

    def reduce_x_end(j):
        for name in ("2a", "2b", "2c", "2d"):
            rs[j, name].wait_recv()
        summed[bs[j]] = (part[j, x].astype(F32) + r2p[j].astype(F32) + r2m[j].astype(F32)).astype(BF16)

    def reduce_z(name):
        if name == "1":
            rz["1a"] = send(summed.at[z2, A], za, up)
            rz["1b"] = send(summed.at[z2, B], zb, down)
        elif name == "2a":
            rz["2a"] = send(summed.at[zu, B], z2p.at[B], up)
        elif name == "2b":
            rz["2b"] = send(summed.at[zd, A], z2m.at[A], down)
        elif name == "2c":
            rz["1a"].wait_recv()
            summed[zu, A] = (summed[zu, A].astype(F32) + za[...].astype(F32)).astype(BF16)
            rz["2c"] = send(summed.at[zu, A], z2p.at[A], up)
        elif name == "2d":
            rz["1b"].wait_recv()
            summed[zd, B] = (summed[zd, B].astype(F32) + zb[...].astype(F32)).astype(BF16)
            rz["2d"] = send(summed.at[zd, B], z2m.at[B], down)

    def weight_grad(q):
        hx[q, "sib"].wait_recv()
        grads = gall[zq[q]].reshape(8 * T, D)
        for m in range(0, FF, 512):
            rows = pl.ds(m, 512)
            block = lax.dot_general(
                hall[zq[q], :, :, :, rows].reshape(8 * T, 512), grads, (((0,), (0,)), ((), ())),
                preferred_element_type=F32,
            )
            if q == 0:
                acc[rows] = block
            elif q < 3:
                acc[rows] += block
            else:
                wg_ref[rows] = (acc[rows] + block).astype(BF16)

    steps = {
        "gy": g_along_y, "gs": g_to_sib, "hz1": h_z_first, "hz2": h_z_second, "hzf": h_z_forward, "hx": h_x, "hxf": h_x_forward, "hs": h_to_sib,
        "p": product, "rx": reduce_x, "rf": reduce_x_forward, "re": reduce_x_end, "rz": reduce_z, "wg": weight_grad,
    }
    for step, *args in ORDER:
        steps[step](*args)

    for copy in (rz["2a"], rz["2b"], rz["2c"], rz["2d"]):
        copy.wait_recv()
    ig_ref[...] = (summed[zh].astype(F32) + z2p[...].astype(F32) + z2m[...].astype(F32)).astype(BF16)
    for copy in started:
        copy.wait_send()


def shards(hidden, weight, out_grad):
    vmem = lambda *shape, dtype=BF16: pltpu.VMEM(shape, dtype)
    return pl.pallas_call(
        kernel,
        name="mlp_backward",
        out_shape=(jax.ShapeDtypeStruct((T, FF), BF16), jax.ShapeDtypeStruct((FF, D), BF16)),
        in_specs=[pl.BlockSpec(memory_space=pl.ANY)] * 3,
        out_specs=[pl.BlockSpec(memory_space=pltpu.VMEM)] * 2,
        scratch_shapes=[
            vmem(4, 4, 2, T, FF),
            vmem(4, 4, 2, T, D),
            vmem(4, 4, T, D),
            vmem(FF, 2 * D),
            vmem(4, 4, T, FF),
            vmem(4, T // 2, FF), vmem(4, T // 2, FF),
            vmem(4, T, FF), vmem(4, T, FF),
            vmem(4, T, FF),
            vmem(T // 2, FF), vmem(T // 2, FF),
            vmem(T, FF), vmem(T, FF),
            vmem(FF, D, dtype=F32),
            pltpu.SemaphoreType.DMA((SENDS,)),
            pltpu.SemaphoreType.DMA((SENDS,)),
            pltpu.SemaphoreType.DMA((3,)),
            pltpu.SemaphoreType.REGULAR,
            pltpu.SemaphoreType.REGULAR,
        ],
        compiler_params=pltpu.CompilerParams(
            collective_id=0, has_side_effects=True, vmem_limit_bytes=48 << 20
        ),
        cost_estimate=pl.CostEstimate(flops=2416 << 20, bytes_accessed=4 << 20, transcendentals=0),
    )(*(pltpu.with_memory_space_constraint(v, pltpu.HBM) for v in (hidden, weight, out_grad.reshape(2, T, D))))


def solution(mesh):
    in_specs = (P("col", "row"), P("row", "col"), P("row", "col"))
    out_specs = (P("col", "row"), P("row", "col"))
    return jax.shard_map(shards, mesh=mesh, in_specs=in_specs, out_specs=out_specs, check_vma=False)
```

time: 75.3 us -> 60.5 us (0.80)
  the two profiles are of different devices: /device:TPU:65 before, /device:TPU:1 now
where the time goes in v2:
time: 60.5 us; the launch traced here: 60.4 us
  Pallas kernels  58.1 us (96%)
  local copies, waits for them, and re-layouts  1.66 us (3%)
  between operations  0.64 us (1%)
    pallas_call x1, Pallas kernels, shards(): pl.pallas_call(kernel, name='mlp_backward', out_shape=(jax.ShapeDtypeStru...  58.1 us
    unnamed x2, local copies, waits for them, and re-layouts  1.66 us

profile of v2, /device:TPU:1, one launch (start us, length us, event | category | flops | bytes accessed | tf_op | source)
XLA Modules:
  0.0 60.4 jit_solution(17750973528214914048)
XLA Ops:
  0.6 58.1 %mlp_backward.1 = (bf16[32,1536]{1,0:T(8,128)(2,1)S(1)}, bf16[1536,384]{1,0:T(8,128)(2,1)S(1)}) custom-call(bf16[32,1536]{1,0:T(8,128)(2,1)} %h_ref.1, bf16[1536,384]{1,0:T(8,128)(2,1)} %w_ref.1, bf16[2,32,384]{2,1,0:T(8,128)(2,1)} %bitcast.1), custom_call_target="tpu_custom_call" | custom-call | flops 2533359616 | bytes 4194304 | tf_op jit(solution)/shard_map/mlp_backward/pallas_call | solution.py:226
  58.7 0.6 %copy.7 = bf16[32,1536]{1,0:T(8,128)(2,1)} copy(bf16[32,1536]{1,0:T(8,128)(2,1)S(1)} %get-tuple-element.4) | data formatting | bytes 196608
  59.4 1.0 %copy.8 = bf16[1536,384]{1,0:T(8,128)(2,1)} copy(bf16[1536,384]{1,0:T(8,128)(2,1)S(1)} %get-tuple-element.5) | data formatting | bytes 2359296

commit v3 on v2

--- a/solution.py
+++ b/solution.py
@@ -8,14 +8,14 @@
 BF16, F32 = jnp.bfloat16, jnp.float32
 FF, D, T = 1536, 384, 32
 A, B = pl.ds(0, T // 2), pl.ds(T // 2, T // 2)
-SENDS = 84
-ORDER = [('hx', 0, 'a'), ('hx', 0, 'b'), ('gy', 1), ('gy', 3), ('gy', 2), ('gs', 0), ('hxf', 0, 'a'), ('hxf', 0, 'b'), ('p', 0), ('rx', 0), ('hz1',), ('gs', 1), ('gs', 3), ('gs', 2), ('rf', 0), ('p', 1), ('rx', 1), ('hzf',), ('hz2',), ('hx', 1, 'a'), ('hx', 2, 'b'), ('p', 2), ('rx', 2), ('re', 0), ('rf', 1), ('hxf', 1, 'a'), ('hxf', 2, 'b'), ('p', 3), ('rx', 3), ('re', 1), ('rz', '1'), ('rf', 2), ('hs', 0), ('hx', 1, 'b'), ('hx', 2, 'a'), ('re', 2), ('rz', '2b'), ('rf', 3), ('hx', 3, 'a'), ('hx', 3, 'b'), ('hxf', 1, 'b'), ('hxf', 2, 'a'), ('re', 3), ('rz', '2a'), ('hs', 1), ('hs', 2), ('wg', 0), ('rz', '2c'), ('rz', '2d'), ('hxf', 3, 'a'), ('hxf', 3, 'b'), ('wg', 1), ('wg', 2), ('hs', 3), ('wg', 3)]
+UNITS, GROUP, SINGLES, RECEIVERS = 75, 15, 9, 48
+ORDER = [('w',), ('gz',), ('gy0',), ('hx', 0, 'b'), ('gy', 3), ('hz1',), ('hx', 0, 'a'), ('gy', 2), ('gy', 1), ('gs', 0), ('hxf', 0, 'a'), ('hxf', 0, 'b'), ('p', 0), ('rxa', 0), ('rxb', 0), ('gs', 1), ('gs', 3), ('hzfb',), ('hzfa',), ('hx', 2, 'b'), ('gs', 2), ('rf', 0), ('hz2',), ('p', 1), ('rxa', 1), ('p', 2), ('rxb', 1), ('rxa', 2), ('re', 0), ('rf', 1), ('p', 3), ('rxa', 3), ('rxb', 3), ('hs', 0), ('re', 1), ('rxb', 2), ('rf', 2), ('rz', '1'), ('wg', 0), ('rf', 3), ('hx', 2, 'a'), ('hx', 3, 'a'), ('re', 2), ('rz', '2b'), ('hx', 1, 'a'), ('hx', 1, 'b'), ('hx', 3, 'b'), ('hxf', 2, 'b'), ('hxf', 2, 'a'), ('re', 3), ('rz', '2a'), ('rz', '2c'), ('rz', '2d'), ('hxf', 1, 'a'), ('hxf', 1, 'b'), ('hxf', 3, 'a'), ('hxf', 3, 'b'), ('hs', 2), ('hs', 1), ('wg', 2), ('hs', 3), ('wg', 1), ('wg', 3)]
 
 
 def kernel(
     h_ref, w_ref, g_ref, ig_ref, wg_ref,
     hall, gall, gsib, wall, part, ra, rb, r2p, r2m, summed, za, zb, z2p, z2m, acc,
-    send_sem, recv_sem, local_sem, near_sem, far_sem,
+    units, send_sem, single_sem, recv_sem, local_sem, near_sem, far_sem,
 ):
     r, c = lax.axis_index("row"), lax.axis_index("col")
     zl, y = r // 4, r % 4
@@ -26,17 +26,33 @@
         col = (((x + dx) % 4) * 4 + (zh + dzh) % 4) * 2 + (k + dk) % 2
         return (row, col)
 
-    started = []
-
-    def send(src, dst, to):
-        i = len(started)
+    sent, singles, receivers = [], [], {}
+
+    def transfer(src, dst, to, wait=None):
+        if wait is None:
+            wait = len(receivers)
+        recv = recv_sem.at[receivers.setdefault(wait, len(receivers))]
+        unit = src.shape[-1] * src.shape[-2] * (src.shape[0] if len(src.shape) > 2 else 1) == T // 2 * FF
+        if unit:
+            sem = send_sem.at[len(sent) // GROUP]
+        else:
+            sem = single_sem.at[len(singles)]
         copy = pltpu.make_async_remote_copy(
-            src_ref=src, dst_ref=dst, send_sem=send_sem.at[i], recv_sem=recv_sem.at[i],
-            device_id=to, device_id_type=pl.DeviceIdType.MESH,
+            src_ref=src, dst_ref=dst, send_sem=sem, recv_sem=recv, device_id=to, device_id_type=pl.DeviceIdType.MESH
         )
+        (sent if unit else singles).append(copy)
+        return copy
+
+    def send(src, dst, to, wait=None):
+        copy = transfer(src, dst, to, wait)
         copy.start()
-        started.append(copy)
         return copy
+
+    def wait_units(semaphore, n):
+        pltpu.make_async_copy(units.at[pl.ds(0, n)], units.at[pl.ds(0, n)], semaphore).wait()
+
+    def wait_all(wait, n=4):
+        wait_units(recv_sem.at[receivers[wait]], n)
 
     load_w = pltpu.make_async_copy(w_ref, wall.at[:, pl.ds(0, D)], local_sem.at[0])
     load_g = pltpu.make_async_copy(g_ref, gall.at[y, zl], local_sem.at[1])
@@ -72,9 +88,7 @@
     xr, xl, x2 = (x + 1) % 4, (x + 3) % 4, (x + 2) % 4
     zu, zd, z2 = (zh + 1) % 4, (zh + 3) % 4, (zh + 2) % 4
 
-    g_zl = {d: send(g_ref, gall.at[y, zl], at(dzl=d)) for d in (1, 3, 2)}
-    g_y = {(0, d): send(g_ref, gall.at[y, zl], at(dy=d)) for d in (1, 3, 2)}
-    w_sib = send(w_ref, wall.at[:, pl.ds(D, D)], sib)
+    g_zl, held = {}, {}
     hx, rs, g_sib, hz, rz = {}, {}, {}, {}, {}
     load_h.wait()
 
@@ -83,18 +97,28 @@
     bs = [y] + [jnp.where(i < at_y, far[i], far[i + 1]) for i in range(3)]
     zq = [zh, zd, zu, z2]
 
+    def g_first():
+        for d in (1, 3, 2):
+            g_zl[d] = send(g_ref, gall.at[y, zl], at(dzl=d))
+
+    def g_first_y():
+        for d in (1, 3, 2):
+            send(g_ref, gall.at[y, zl], at(dy=d), f"gy{d}")
+
+    def w_to_sib():
+        held["w"] = send(w_ref, wall.at[:, pl.ds(D, D)], sib)
+
     def g_along_y(d):
         g_zl[d].wait_recv()
         block = gall.at[y, (zl - d + 4) % 4]
         for dy in (1, 3, 2):
-            g_y[d, dy] = send(block, block, at(dy=dy))
+            send(block, block, at(dy=dy), f"gy{dy}")
 
     def g_to_sib(d):
         if d == 0:
             load_g.wait()
         else:
-            for e in (0, 1, 3, 2):
-                g_y[e, d].wait_recv()
+            wait_all(f"gy{d}")
         b = (y - d + 4) % 4
         g_sib[d] = send(gall.at[b, :, 1 - k], gsib.at[b], sib)
 
@@ -115,9 +139,11 @@
         hz["2u"] = send(h_ref.at[B], hall.at[zh, x, k, B], up)
         hz["2d"] = send(h_ref.at[A], hall.at[zh, x, k, A], down)
 
-    def h_z_forward():
+    def h_z_forward_up():
         hz["1u"].wait_recv()
         hz["fa"] = send(hall.at[zd, x, k, A], hall.at[zd, x, k, A], up)
+
+    def h_z_forward_down():
         hz["1d"].wait_recv()
         hz["fb"] = send(hall.at[zu, x, k, B], hall.at[zu, x, k, B], down)
 
@@ -126,24 +152,23 @@
         if after:
             hz[after].wait_recv()
         block = hall.at[zq[q], x, k, A if name == "a" else B]
-        hx[q, name, "r"] = send(block, block, right)
-        hx[q, name, "l"] = send(block, block, left)
+        hx[q, name, "r"] = send(block, block, right, None if name == "a" else f"hx{q}")
+        hx[q, name, "l"] = send(block, block, left, None if name == "b" else f"hx{q}")
 
     def h_x_forward(q, name):
         hx[q, name, "r" if name == "a" else "l"].wait_recv()
         block = hall.at[zq[q], xl, k, A] if name == "a" else hall.at[zq[q], xr, k, B]
-        hx[q, "f" + name] = send(block, block, right if name == "a" else left)
+        send(block, block, right if name == "a" else left, f"hx{q}")
 
     def h_to_sib(q):
-        for name in ((q, "b", "r"), (q, "a", "l"), (q, "fa"), (q, "fb")):
-            hx[name].wait_recv()
+        wait_all(f"hx{q}")
         block = hall.at[zq[q], :, k]
         hx[q, "sib"] = send(block, block, sib)
 
     def product(j):
         if j == 0:
             load_w.wait()
-            w_sib.wait_recv()
+            held["w"].wait_recv()
             g_sib[0].wait_recv()
         if j == 1:
             for d in (1, 3, 2):
@@ -155,23 +180,24 @@
             block = lax.dot_general(grads, wall[cols], (((1,), (1,)), ((), ())), preferred_element_type=F32)
             part[j, :, :, cols] = block.astype(BF16).reshape(4, T, 512)
 
-    def reduce_x(j):
+    def reduce_x_far(j):
         rs[j, "1a"] = send(part.at[j, x2, A], ra.at[j], right)
         rs[j, "1b"] = send(part.at[j, x2, B], rb.at[j], left)
-        rs[j, "2a"] = send(part.at[j, xr, B], r2p.at[j, B], right)
-        rs[j, "2b"] = send(part.at[j, xl, A], r2m.at[j, A], left)
+
+    def reduce_x_near(j):
+        send(part.at[j, xr, B], r2p.at[j, B], right, f"rs{j}")
+        send(part.at[j, xl, A], r2m.at[j, A], left, f"rs{j}")
 
     def reduce_x_forward(j):
         rs[j, "1a"].wait_recv()
         part[j, xr, A] = (part[j, xr, A].astype(F32) + ra[j].astype(F32)).astype(BF16)
-        rs[j, "2c"] = send(part.at[j, xr, A], r2p.at[j, A], right)
+        send(part.at[j, xr, A], r2p.at[j, A], right, f"rs{j}")
         rs[j, "1b"].wait_recv()
         part[j, xl, B] = (part[j, xl, B].astype(F32) + rb[j].astype(F32)).astype(BF16)
-        rs[j, "2d"] = send(part.at[j, xl, B], r2m.at[j, B], left)
+        send(part.at[j, xl, B], r2m.at[j, B], left, f"rs{j}")
 
     def reduce_x_end(j):
-        for name in ("2a", "2b", "2c", "2d"):
-            rs[j, name].wait_recv()
+        wait_all(f"rs{j}")
         summed[bs[j]] = (part[j, x].astype(F32) + r2p[j].astype(F32) + r2m[j].astype(F32)).astype(BF16)
 
     def reduce_z(name):
@@ -179,17 +205,17 @@
             rz["1a"] = send(summed.at[z2, A], za, up)
             rz["1b"] = send(summed.at[z2, B], zb, down)
         elif name == "2a":
-            rz["2a"] = send(summed.at[zu, B], z2p.at[B], up)
+            send(summed.at[zu, B], z2p.at[B], up, "rz")
         elif name == "2b":
-            rz["2b"] = send(summed.at[zd, A], z2m.at[A], down)
+            send(summed.at[zd, A], z2m.at[A], down, "rz")
         elif name == "2c":
             rz["1a"].wait_recv()
             summed[zu, A] = (summed[zu, A].astype(F32) + za[...].astype(F32)).astype(BF16)
-            rz["2c"] = send(summed.at[zu, A], z2p.at[A], up)
+            send(summed.at[zu, A], z2p.at[A], up, "rz")
         elif name == "2d":
             rz["1b"].wait_recv()
             summed[zd, B] = (summed[zd, B].astype(F32) + zb[...].astype(F32)).astype(BF16)
-            rz["2d"] = send(summed.at[zd, B], z2m.at[B], down)
+            send(summed.at[zd, B], z2m.at[B], down, "rz")
 
     def weight_grad(q):
         hx[q, "sib"].wait_recv()
@@ -208,16 +234,17 @@
                 wg_ref[rows] = (acc[rows] + block).astype(BF16)
 
     steps = {
-        "gy": g_along_y, "gs": g_to_sib, "hz1": h_z_first, "hz2": h_z_second, "hzf": h_z_forward, "hx": h_x, "hxf": h_x_forward, "hs": h_to_sib,
-        "p": product, "rx": reduce_x, "rf": reduce_x_forward, "re": reduce_x_end, "rz": reduce_z, "wg": weight_grad,
+        "gy": g_along_y, "gs": g_to_sib, "hz1": h_z_first, "hz2": h_z_second, "hzfa": h_z_forward_up, "hzfb": h_z_forward_down, "hx": h_x, "hxf": h_x_forward, "hs": h_to_sib,
+        "p": product, "rxa": reduce_x_far, "rxb": reduce_x_near, "gz": g_first, "gy0": g_first_y, "w": w_to_sib, "rf": reduce_x_forward, "re": reduce_x_end, "rz": reduce_z, "wg": weight_grad,
     }
     for step, *args in ORDER:
         steps[step](*args)
 
-    for copy in (rz["2a"], rz["2b"], rz["2c"], rz["2d"]):
-        copy.wait_recv()
+    wait_all("rz")
     ig_ref[...] = (summed[zh].astype(F32) + z2p[...].astype(F32) + z2m[...].astype(F32)).astype(BF16)
-    for copy in started:
+    for group in range(UNITS // GROUP):
+        wait_units(send_sem.at[group], GROUP)
+    for copy in singles:
         copy.wait_send()
 
 
@@ -241,8 +268,10 @@
             vmem(T // 2, FF), vmem(T // 2, FF),
             vmem(T, FF), vmem(T, FF),
             vmem(FF, D, dtype=F32),
-            pltpu.SemaphoreType.DMA((SENDS,)),
-            pltpu.SemaphoreType.DMA((SENDS,)),
+            vmem(GROUP, T // 2, FF),
+            pltpu.SemaphoreType.DMA((UNITS // GROUP,)),
+            pltpu.SemaphoreType.DMA((SINGLES,)),
+            pltpu.SemaphoreType.DMA((RECEIVERS,)),
             pltpu.SemaphoreType.DMA((3,)),
             pltpu.SemaphoreType.REGULAR,
             pltpu.SemaphoreType.REGULAR,

time: 60.5 us -> 55.7 us (0.921)
  Pallas kernels: 58.1 us -> 53 us
    pallas_call x1, Pallas kernels: 58.1 us -> 53 us  [shards(): pl.pallas_call(kernel, name='mlp_backward', out_shape=(jax.ShapeDtypeStru...]
where the time goes in v3:
time: 55.7 us; the launch traced here: 55.3 us
  Pallas kernels  53 us (95%)
  local copies, waits for them, and re-layouts  1.66 us (3%)
  between operations  0.64 us (1%)
    pallas_call x1, Pallas kernels, shards(): pl.pallas_call(kernel, name='mlp_backward', out_shape=(jax.ShapeDtypeStru...  53 us
    unnamed x2, local copies, waits for them, and re-layouts  1.66 us

profile of v3, /device:TPU:1, one launch (start us, length us, event | category | flops | bytes accessed | tf_op | source)
XLA Modules:
  0.0 55.3 jit_solution(17725744665310837056)
XLA Ops:
  0.6 53.0 %mlp_backward.1 = (bf16[32,1536]{1,0:T(8,128)(2,1)S(1)}, bf16[1536,384]{1,0:T(8,128)(2,1)S(1)}) custom-call(bf16[32,1536]{1,0:T(8,128)(2,1)} %h_ref.1, bf16[1536,384]{1,0:T(8,128)(2,1)} %w_ref.1, bf16[2,32,384]{2,1,0:T(8,128)(2,1)} %bitcast.1), custom_call_target="tpu_custom_call" | custom-call | flops 2533359616 | bytes 4194304 | tf_op jit(solution)/shard_map/mlp_backward/pallas_call | solution.py:253
  53.6 0.6 %copy.7 = bf16[32,1536]{1,0:T(8,128)(2,1)} copy(bf16[32,1536]{1,0:T(8,128)(2,1)S(1)} %get-tuple-element.4) | data formatting | bytes 196608
  54.2 1.0 %copy.8 = bf16[1536,384]{1,0:T(8,128)(2,1)} copy(bf16[1536,384]{1,0:T(8,128)(2,1)S(1)} %get-tuple-element.5) | data formatting | bytes 2359296

commit v4 on v3

--- a/solution.py
+++ b/solution.py
@@ -9,7 +9,16 @@
 FF, D, T = 1536, 384, 32
 A, B = pl.ds(0, T // 2), pl.ds(T // 2, T // 2)
 UNITS, GROUP, SINGLES, RECEIVERS = 75, 15, 9, 48
-ORDER = [('w',), ('gz',), ('gy0',), ('hx', 0, 'b'), ('gy', 3), ('hz1',), ('hx', 0, 'a'), ('gy', 2), ('gy', 1), ('gs', 0), ('hxf', 0, 'a'), ('hxf', 0, 'b'), ('p', 0), ('rxa', 0), ('rxb', 0), ('gs', 1), ('gs', 3), ('hzfb',), ('hzfa',), ('hx', 2, 'b'), ('gs', 2), ('rf', 0), ('hz2',), ('p', 1), ('rxa', 1), ('p', 2), ('rxb', 1), ('rxa', 2), ('re', 0), ('rf', 1), ('p', 3), ('rxa', 3), ('rxb', 3), ('hs', 0), ('re', 1), ('rxb', 2), ('rf', 2), ('rz', '1'), ('wg', 0), ('rf', 3), ('hx', 2, 'a'), ('hx', 3, 'a'), ('re', 2), ('rz', '2b'), ('hx', 1, 'a'), ('hx', 1, 'b'), ('hx', 3, 'b'), ('hxf', 2, 'b'), ('hxf', 2, 'a'), ('re', 3), ('rz', '2a'), ('rz', '2c'), ('rz', '2d'), ('hxf', 1, 'a'), ('hxf', 1, 'b'), ('hxf', 3, 'a'), ('hxf', 3, 'b'), ('hs', 2), ('hs', 1), ('wg', 2), ('hs', 3), ('wg', 1), ('wg', 3)]
+ORDER = [
+    ("gz",), ("w",), ("gy0",), ("hx", 0, "b"), ("gy", 3), ("hz1",), ("hx", 0, "a"), ("gy", 2), ("gy", 1), ("gs", 0),
+    ("hxf", 0, "a"), ("hxf", 0, "b"), ("p", 0), ("rxa", 0), ("rxb", 0), ("gs", 1), ("gs", 3), ("hzfb",), ("hzfa",),
+    ("hx", 2, "b"), ("gs", 2), ("rf", 0), ("hz2",), ("p", 1), ("rxa", 1), ("p", 2), ("rxb", 1), ("rxa", 2), ("rf", 1),
+    ("p", 3), ("re", 0), ("rxa", 3), ("rxb", 3), ("hs", 0), ("re", 1), ("rxb", 2), ("rf", 2), ("rz", "1"), ("wg", 0),
+    ("rf", 3), ("hx", 2, "a"), ("re", 2), ("rz", "2b"), ("hx", 1, "a"), ("hx", 1, "b"), ("hx", 3, "b"), ("hxf", 2,
+    "b"), ("hx", 3, "a"), ("hxf", 2, "a"), ("re", 3), ("rz", "2a"), ("rz", "2d"), ("rz", "2c"), ("hxf", 1, "a"),
+    ("hxf", 1, "b"), ("hxf", 3, "b"), ("hxf", 3, "a"), ("hs", 2), ("hs", 1), ("wg", 2), ("hs", 3), ("wg", 1), ("wg",
+    3),
+]
 
 
 def kernel(

time: 55.7 us -> 55.5 us (level)
  the two profiles are of different devices: /device:TPU:1 before, /device:TPU:89 now
where the time goes in v4:
time: 55.5 us; the launch traced here: 55.4 us
  Pallas kernels  53.1 us (96%)
  local copies, waits for them, and re-layouts  1.66 us (3%)
  between operations  0.64 us (1%)
    pallas_call x1, Pallas kernels, shards(): pl.pallas_call(kernel, name='mlp_backward', out_shape=(jax.ShapeDtypeStru...  53.1 us
    unnamed x2, local copies, waits for them, and re-layouts  1.66 us

profile of v4, /device:TPU:89, one launch (start us, length us, event | category | flops | bytes accessed | tf_op | source)
XLA Modules:
  0.0 55.4 jit_solution(2530971941910332973)
XLA Ops:
  0.6 53.1 %mlp_backward.1 = (bf16[32,1536]{1,0:T(8,128)(2,1)S(1)}, bf16[1536,384]{1,0:T(8,128)(2,1)S(1)}) custom-call(bf16[32,1536]{1,0:T(8,128)(2,1)} %h_ref.1, bf16[1536,384]{1,0:T(8,128)(2,1)} %w_ref.1, bf16[2,32,384]{2,1,0:T(8,128)(2,1)} %bitcast.1), custom_call_target="tpu_custom_call" | custom-call | flops 2533359616 | bytes 4194304 | tf_op jit(solution)/shard_map/mlp_backward/pallas_call | solution.py:262
  53.7 0.6 %copy.7 = bf16[32,1536]{1,0:T(8,128)(2,1)} copy(bf16[32,1536]{1,0:T(8,128)(2,1)S(1)} %get-tuple-element.4) | data formatting | bytes 196608
  54.4 1.0 %copy.8 = bf16[1536,384]{1,0:T(8,128)(2,1)} copy(bf16[1536,384]{1,0:T(8,128)(2,1)S(1)} %get-tuple-element.5) | data formatting | bytes 2359296
